TPU v7x, 256 devices: a whole 4x4x8 slice. The times are simulated.
256 devices in a mesh: dp: 16 (over z, core), expert: 16 (over y, x).
Axes of the slice: x: 4, y: 4, z: 8, core: 2. Of those that a mesh axis runs over, the one named last changes fastest.
Arguments:
- dy_tokens: bfloat16 [131072, 4096], P(('dp', 'expert')), may hold values from -6 to 6
- gates: bfloat16 [131072, 8], P(('dp', 'expert')), may hold values from 0.049804688 to 1
- routes: int32 [131072, 8], P(('dp', 'expert')), may hold values from 0 to 127, as said below
- hidden: bfloat16 [16, 16384, 1536], P('expert', 'dp'), may hold values from -6 to 6
- projector: bfloat16 [16, 1536, 256], P('expert'), may hold values from -0.15625 to 0.15625
- weights: bfloat16 [16, 1536, 4096], P('expert', None, 'dp'), may hold values from -0.15625 to 0.15625
- moment_one: float32 [4096, 16, 256], P('dp', 'expert'), may hold values from -6 to 6
- moment_two: float32 [4096, 16, 256], P('dp', 'expert'), may hold values from 0.25 to 4
Outputs:
- new_weights: bfloat16 [16, 1536, 4096], P('expert', None, 'dp')
- new_moment_one: float32 [4096, 16, 256], P('dp', 'expert')
- new_moment_two: float32 [4096, 16, 256], P('dp', 'expert')
Inputs may be any that keep to these rules, and one draw needn't show every extreme that they name: `routes`: each row names 8 different experts, one from each group of 16 consecutive ids, so exactly one below 16; among the 512 rows of one device no expert below 16 is named more than 64 times, and some such expert exactly 64 times.
All inputs are finite; a program needn't handle non-finite values.
Results may differ from a plain program's by a relative error of at most 0.0035.
Values may be sent and summed in bfloat16 or wider, within the bound.
A program may use at most 192 MiB of HBM per device.

v0:
```python
import jax
import jax.numpy as jnp
from jax import lax
from jax.sharding import PartitionSpec as P

EXPERTS = 16


grad_scale = 1.0
beta_one = 0.9
beta_two = 0.999
eps = 1e-06
step_size = 0.02


def pack_rows(dy_tokens, gates, onehot, member, rank, capacity):
    tok_rows = dy_tokens.shape[0]
    weight = jnp.sum(jnp.where(onehot, gates.astype(jnp.float32)[:, :, None], 0.0), axis=1)
    positions = jnp.arange(capacity, dtype=jnp.int32)
    select = (rank.T[:, None, :] == positions[None, :, None]) & (member.T[:, None, :] > 0)
    order = jnp.arange(tok_rows, dtype=jnp.int32)
    taken = jnp.sum(jnp.where(select, order[None, None, :], 0), axis=2)
    filled = jnp.any(select, axis=2)
    factor = jnp.where(filled, jnp.take_along_axis(weight.T, taken, axis=1), 0.0)
    return (dy_tokens[taken] * factor[:, :, None]).astype(jnp.bfloat16)


def body(dy_tokens, gates, routes, hidden, projector, weights, moment_one, moment_two):
    tok_rows, width = dy_tokens.shape
    local_experts = hidden.shape[0]
    groups = lax.axis_size("expert")
    capacity = hidden.shape[1] // groups
    feature_width = hidden.shape[2]
    labels = jnp.arange(EXPERTS, dtype=jnp.int32)
    onehot = routes[:, :, None] == labels[None, None, :]
    member = jnp.sum(onehot.astype(jnp.int32), axis=1)
    rank = jnp.cumsum(member, axis=0) - 1
    packed = pack_rows(dy_tokens, gates, onehot, member, rank, capacity)
    slot_blocks = hidden.reshape(local_experts, groups, capacity, feature_width)
    reduced = jnp.einsum(
        "jscf,jfr->jscr", slot_blocks, projector, preferred_element_type=jnp.float32
    ).astype(jnp.bfloat16)
    outgoing = packed.reshape(groups, local_experts, capacity, width)
    arrived = lax.all_to_all(outgoing, "expert", split_axis=0, concat_axis=0, tiled=True)
    grads = jnp.einsum("sjcd,jscr->djr", arrived, reduced, preferred_element_type=jnp.float32)
    owned_rows = moment_one.shape[0]
    summed = lax.psum(grads, "dp")
    share = lax.dynamic_slice_in_dim(summed, lax.axis_index("dp") * owned_rows, owned_rows, 0)
    grad = share * grad_scale
    new_one = beta_one * moment_one + (1.0 - beta_one) * grad
    new_two = beta_two * moment_two + (1.0 - beta_two) * grad * grad
    direction = (new_one / (jnp.sqrt(new_two) + eps)).astype(jnp.bfloat16)
    update = jnp.einsum("jfr,djr->jfd", projector, direction, preferred_element_type=jnp.float32)
    new_weights = (weights.astype(jnp.float32) - step_size * update).astype(jnp.bfloat16)
    return (new_weights, new_one, new_two)


def solution(mesh):
    in_specs = (
        P(("dp", "expert"), None),
        P(("dp", "expert"), None),
        P(("dp", "expert"), None),
        P("expert", "dp", None),
        P("expert", None, None),
        P("expert", None, "dp"),
        P("dp", "expert", None),
        P("dp", "expert", None),
    )
    out_specs = (P("expert", None, "dp"), P("dp", "expert", None), P("dp", "expert", None))
    return jax.shard_map(body, mesh=mesh, in_specs=in_specs, out_specs=out_specs, check_vma=False)
```

profile of v0, /device:TPU:1, one launch (start us, length us, event | category | flops | bytes accessed | tf_op | source)
XLA Modules:
  0.0 299.4 jit_solution(14779287297246577191)
XLA Ops:
  7.2 0.0 copy-start
  7.2 0.0 all-reduce.2.cloned.1.call-start
  7.2 0.9 convert_reduce_fusion
  8.2 1.2 reduce-window.6
  9.3 0.2 slice_reduce_fusion
  9.6 0.1 copy_bitcast_fusion
  9.6 0.5 select_reduce_fusion
  10.2 0.4 fusion.10
  10.6 0.1 reshape.107
  10.7 0.7 convert_element_type.47
  11.4 0.8 select_reduce_fusion.1
  12.2 0.1 copy.45
  12.3 7.3 %gather_fusion.1 = f32[1024]{0:T(1024)S(1)} fusion(f32[16,512]{0,1:T(8,128)S(1)} %bitcast.57, s32[1024]{0:T(1024)S(1)} %reshape.107), kind=kCustom, calls=%fused_computation.1 | custom fusion | bytes 16384 | tf_op jit(solution)/shard_map/jit(take_along_axis)/gather | solution.py:24
  19.6 0.1 reshape.110
  19.7 0.1 reshape.101
  19.7 17.8 %gather_fusion = bf16[1024,4096]{1,0:T(8,128)(2,1)} fusion(bf16[512,4096]{1,0:T(8,128)(2,1)} %param.8, s32[1024]{0:T(1024)S(1)} %broadcast_clamp_fusion), kind=kCustom, calls=%fused_computation | custom fusion | bytes 16781312 | tf_op jit(solution)/shard_map/gather | solution.py:25
  37.6 10.0 %fusion = bf16[16,1,64,4096]{3,2,1,0:T(8,128)(2,1)} fusion(bf16[16,1,64,4096]{3,2,1,0:T(8,128)(2,1)} %bitcast.58, f32[16,64]{1,0:T(8,128)S(1)} %select_select_fusion), kind=kLoop, calls=%fused_computation.3 | loop fusion | flops 12582912 | bytes 16781312 | tf_op jit(solution)/shard_map/convert_element_type | solution.py:25
  47.5 102.5 %all_to_all.5 = bf16[16,1,64,4096]{3,2,1,0:T(8,128)(2,1)} all-to-all(bf16[16,1,64,4096]{3,2,1,0:T(8,128)(2,1)} %fusion), channel_id=1, replica_groups=mesh['dp'=16,'expert'=16] {'expert'}, dimensions={0} | all-to-all | bytes 16777216 | tf_op jit(solution)/shard_map/all_to_all | solution.py:44
  150.0 0.0 copy-done
  150.0 10.4 %fusion.3 = f32[4096,1,256]{0,2,1:T(8,128)} fusion(bf16[16,1,64,4096]{3,2,1,0:T(8,128)(2,1)} %all_to_all.5, bf16[16,64,1536]{2,1,0:T(8,128)(2,1)S(1)} %bitcast.56, bf16[1,1536,256]{2,1,0:T(8,128)(2,1)} %param.12), kind=kOutput, calls=%fused_computation.6 | convolution fusion | flops 2953052160 | bytes 16515072 | tf_op jit(solution)/shard_map/sjcd,jscr->djr/dot_general | solution.py:45
  160.4 0.0 all-reduce.2.cloned.1.call-update
  160.4 1.1 copy.42
  161.5 1.8 copy.47
  163.3 2.3 copy.41
  165.6 116.3 %all-reduce.2.cloned.1.call-done = f32[4096,1,256]{0,2,1:T(8,128)} async-done(((f32[4096,1,256]{0,2,1:T(8,128)}), f32[4096,1,256]{0,2,1:T(8,128)}) %all-reduce.2.cloned.1.call-update) | async-done | bytes 4194320 | tf_op jit(solution)/shard_map/psum | solution.py:47
  281.9 1.9 fusion.14
  283.8 1.8 copy.49
  285.6 1.8 copy.50
  287.4 2.9 fusion.8
  290.3 2.3 copy.48
  (7 shorter events, 0.1 us)
Async XLA Ops:
  7.2 142.8 %copy-start = (bf16[1,1024,1536]{2,1,0:T(8,128)(2,1)S(1)}, bf16[1,1024,1536]{2,1,0:T(8,128)(2,1)}, u32[]{:S(2)}) copy-start(bf16[1,1024,1536]{2,1,0:T(8,128)(2,1)} %param.11) | copy-start | bytes 9437188
  7.2 274.7 %all-reduce.2.cloned.1.call-start = ((), (), s32[]{:S(2)}) async-start(), calls=%async_computation.1 | async-start | bytes 8388608 | tf_op jit(solution)/shard_map/psum | solution.py:47
Sparse Core Ops, SparseCore 0:
  160.5 121.3 all-reduce.1
where the time goes:
time: 300 us; the launch traced here: 299 us
  waiting for transfers between devices  116 us (39%)
  blocking collectives  102 us (34%)
  local copies, waits for them, and re-layouts  36.7 us (12%)
  other arithmetic  16.5 us (6%)
  between operations  14.1 us (5%)
  matrix products  13.3 us (4%)
    psum x1, waiting for transfers between devices, body(): summed = lax.psum(grads, 'dp')  116 us
    all_to_all x1, blocking collectives, body(): lax.all_to_all(outgoing, 'expert', split_axis=0, concat_axis=0, tiled=True)  102 us
    gather x1, local copies, waits for them, and re-layouts, pack_rows(): return (dy_tokens[taken] * factor[:, :, None]).astype(jnp.bfloat16)  17.8 us
    unnamed x8, local copies, waits for them, and re-layouts  11 us
    dot_general x1, matrix products, body(): jnp.einsum('sjcd,jscr->djr', arrived, reduced, preferred_element_type=jnp...  10.4 us
    convert_element_type x1, other arithmetic, pack_rows(): return (dy_tokens[taken] * factor[:, :, None]).astype(jnp.bfloat16)  9.97 us
    gather x3, local copies, waits for them, and re-layouts, pack_rows(): jnp.take_along_axis(weight.T, taken, axis=1)  7.43 us
  transfers between devices with their start and end apart: 1, of which 1 were waited for; matrix products, arithmetic and copies ran while one was open for 2% of the time, Pallas kernels for 0%

commit v1 on v0

v1 whole, which is shorter than its diff:
```python
import jax
import jax.numpy as jnp
from jax import lax
from jax.experimental import pallas as pl
from jax.experimental.pallas import tpu as pltpu
from jax.sharding import PartitionSpec as P

EXPERTS = 16
CAP = 64
GX, GY, GZ = 4, 4, 8
MESH = pl.DeviceIdType.MESH

beta_one = 0.9
beta_two = 0.999
eps = 1e-06
step_size = 0.02

F32, BF16 = jnp.float32, jnp.bfloat16


def dot(a, b):
    return jnp.dot(a, b, preferred_element_type=F32)


def dot_nt(a, b):
    return lax.dot_general(a, b, (((1,), (1,)), ((), ())), preferred_element_type=F32)


def eye(n):
    same = lax.broadcasted_iota(jnp.int32, (n, n), 0) == lax.broadcasted_iota(jnp.int32, (n, n), 1)
    return jnp.where(same, 1.0, 0.0).astype(BF16)


def grad_kernel(
    dy, routes, gates, hidden, projector, grad,
    dyb, hid, proj, pmat, pk, rl, ra, rt, rx, zs, zr, fs, fr,
    load_sem, dy_sem, r_send, r_recv, pk_send, rx_recv, z_send, z_recv, f_send, f_recv,
):
    dp, ex = lax.axis_index("dp"), lax.axis_index("expert")
    x, y, z, c = ex % GX, ex // GX, dp // 2, dp % 2

    def dev(x, y, z, c):
        return (z * 2 + c, y * GX + x)

    def remote(src, dst, send, recv, to):
        return pltpu.make_async_remote_copy(src, dst, send, recv, device_id=to, device_id_type=MESH)

    row = [(dx, 0, dc) for dx in range(GX) for dc in range(2)]
    col = [(0, ddy, dc) for ddy in range(GY) for dc in range(2)]

    def far(s):
        return (8 - s) // 2

    def slab(s):
        return (z + jnp.where(s % 2 == 0, far(s), GZ - far(s))) % GZ

    def load_dy(s):
        width = dyb.shape[2]
        return pltpu.make_async_copy(
            dy.at[:, pl.ds(pl.multiple_of(slab(s) * width, width), width)], dyb.at[s], dy_sem.at[s]
        )

    load_hid = pltpu.make_async_copy(hidden, hid, load_sem.at[0])
    load_proj = pltpu.make_async_copy(projector, proj, load_sem.at[1])
    load_proj.start()
    load_hid.start()

    @pl.loop(0, GZ)
    def _(s):
        load_dy(s).start()

    barrier = pltpu.get_barrier_semaphore()
    partners = [dev((x + a) % GX, (y + b) % GY, z, (c + d) % 2) for a, b, d in row[1:] + col[2:]]
    partners += [dev(x, y, (z + 1) % GZ, c), dev(x, y, (z + GZ - 1) % GZ, c)]
    for to in partners:
        pl.semaphore_signal(barrier, inc=1, device_id=to, device_id_type=MESH)

    zr[0, 3, 1] = jnp.zeros(zr.shape[3:], BF16)
    zr[1, 3, 0] = jnp.zeros(zr.shape[3:], BF16)

    tokens = routes.shape[1]
    ids = routes[...]
    here = ids < EXPERTS
    expert = jnp.sum(jnp.where(here, ids, 0), axis=0, keepdims=True)
    gate = jnp.sum(jnp.where(here, gates[...].astype(F32), 0.0), axis=0, keepdims=True)
    chosen = lax.broadcasted_iota(jnp.int32, (EXPERTS, tokens), 0) == expert
    earlier = lax.broadcasted_iota(jnp.int32, (tokens, tokens), 0) < lax.broadcasted_iota(
        jnp.int32, (tokens, tokens), 1
    )
    count = dot(jnp.where(chosen, 1.0, 0.0).astype(BF16), jnp.where(earlier, 1.0, 0.0).astype(BF16))
    rank = jnp.sum(jnp.where(chosen, count, 0.0), axis=0, keepdims=True).astype(jnp.int32)
    slot = expert * CAP + rank
    for e in range(0, EXPERTS, 4):
        at = lax.broadcasted_iota(jnp.int32, (4 * CAP, tokens), 0) + e * CAP
        pmat[e * CAP : (e + 4) * CAP, :] = jnp.where(at == slot, gate, 0.0).astype(BF16)

    load_proj.wait()
    load_hid.wait()
    for b in range(GY):
        rows = GX * CAP
        part = dot(hid[b * rows : (b + 1) * rows, :], proj[...]).astype(BF16)
        rl[b] = part.reshape(GX, CAP, part.shape[1])

    pl.semaphore_wait(barrier, len(partners))

    def reduced_copy(h, k):
        if h == 0:
            to = (y + k) % GY
            return rl.at[to], ra.at[0, y % 2, c], r_send.at[h, k], r_recv.at[h, y % 2, c], dev(x, to, z, y // 2)
        to = (x + k) % GX
        return rl.at[:, to], ra.at[1, x % 2, c], r_send.at[h, k], r_recv.at[h, x % 2, c], dev(to, y, z, x // 2)

    stays = [y // 2 == c, x // 2 == c]
    for k in range(4):
        for h in range(2):
            src, dst, ss, rs, to = reduced_copy(h, k)
            if k:
                remote(src, dst, ss, rs, to).start()
            else:
                pl.when(stays[h])(lambda: pltpu.make_async_copy(src, dst, rs).start())
                pl.when(jnp.logical_not(stays[h]))(lambda: remote(src, dst, ss, rs, to).start())

    def row_copy(s, h, n):
        if h == 0:
            dx, _, dc = row[n]
            tx, tc = (x + dx) % GX, (c + dc) % 2
            return pk.at[s, 0, pl.ds(2 * tc, 2), tx], rx.at[s, 0, :, c, x], dev(tx, y, z, tc)
        _, ddy, dc = col[n]
        ty, tc = (y + ddy) % GY, (c + dc) % 2
        return pk.at[s, 1, ty, pl.ds(2 * tc, 2)], rx.at[s, 1, :, c, y], dev(x, ty, z, tc)

    @pl.loop(0, GZ)
    def _(s):
        load_dy(s).wait()
        packed = dot(pmat[...], dyb[s]).astype(BF16)
        half = packed.shape[1] // 2
        for h in range(2):
            pk[s, h] = packed[:, h * half : (h + 1) * half].reshape(GY, GX, CAP, half)
        for n in range(8):
            for h in range(2):
                src, dst, to = row_copy(s, h, n)
                if n:
                    remote(src, dst, pk_send.at[s, h, n], rx_recv.at[s, h], to).start()
                else:
                    pltpu.make_async_copy(src, dst, rx_recv.at[s, h]).start()

    def landed(buf, sem):
        pltpu.make_async_copy(buf, buf, sem).wait()

    for h in range(2):
        for e in range(2):
            for k in range(2):
                landed(ra.at[h, e, k], r_recv.at[h, e, k])
            got = ra[h, e].reshape(8 * CAP, ra.shape[-1])
            rt[h, e] = dot_nt(eye(got.shape[1]), got).astype(BF16)

    def partial(s, h, e):
        got = rx[s, h, e]
        return dot(rt[h, e], got.reshape(8 * CAP, got.shape[-1]))

    def z_copy(s, h, e, way, k):
        to = dev(x, y, (z + jnp.where(way == 0, 1, GZ - 1)) % GZ, c)
        return remote(
            zs.at[s, h, e], zr.at[way, k - 1, h, e], z_send.at[s, h, e], z_recv.at[way, k - 1, h, e], to
        )

    for h in range(2):
        landed(rx.at[0, h], rx_recv.at[0, h])
        for e in range(2):
            zs[0, h, e] = partial(0, h, e).astype(BF16)
            z_copy(0, h, e, h, 4).start()

    @pl.loop(1, 7)
    def _(s):
        way, k = s % 2, far(s)
        for h in range(2):
            landed(rx.at[s, h], rx_recv.at[s, h])
            for e in range(2):
                total = partial(s, h, e)

                @pl.when(s != h + 1)
                def _():
                    landed(zr.at[way, k, h, e], z_recv.at[way, k, h, e])

                zs[s, h, e] = (total + zr[way, k, h, e].astype(F32)).astype(BF16)
                z_copy(s, h, e, way, k).start()

    def owner_copy(h, e):
        to = 2 * c + e
        if h == 0:
            return fs.at[0, e], fr.at[y], f_send.at[h, e], f_recv.at[y], dev(x, to, z, 0), (to == y) & (c == 0)
        return fs.at[1, e], fr.at[x], f_send.at[h, e], f_recv.at[x], dev(to, y, z, 1), (to == x) & (c == 1)

    for h in range(2):
        landed(rx.at[7, h], rx_recv.at[7, h])
        for e in range(2):
            total = partial(7, h, e)
            for way in range(2):
                landed(zr.at[way, 0, h, e], z_recv.at[way, 0, h, e])
                total = total + zr[way, 0, h, e].astype(F32)
            fs[h, e] = total.astype(BF16)
            src, dst, ss, rs, to, own = owner_copy(h, e)
            pl.when(own)(lambda: pltpu.make_async_copy(src, dst, rs).start())
            pl.when(jnp.logical_not(own))(lambda: remote(src, dst, ss, rs, to).start())

    for k in range(4):
        landed(fr.at[k], f_recv.at[k])
    total = fr[0].astype(F32)
    for k in range(1, 4):
        total = total + fr[k].astype(F32)
    grad[...] = total.T

    for h in range(2):
        for k in range(4):
            src, dst, ss, rs, to = reduced_copy(h, k)
            if k:
                remote(src, dst, ss, rs, to).wait_send()
            else:
                pl.when(jnp.logical_not(stays[h]))(lambda: remote(src, dst, ss, rs, to).wait_send())
        for e in range(2):
            src, dst, ss, rs, to, own = owner_copy(h, e)
            pl.when(jnp.logical_not(own))(lambda: remote(src, dst, ss, rs, to).wait_send())

    @pl.loop(0, GZ)
    def _(s):
        for h in range(2):
            for n in range(1, 8):
                src, dst, to = row_copy(s, h, n)
                remote(src, dst, pk_send.at[s, h, n], rx_recv.at[s, h], to).wait_send()

    @pl.loop(0, 7)
    def _(s):
        for h in range(2):
            for e in range(2):
                z_copy(s, h, e, 0, 1).wait_send()


def grads(dy, routes, gates, hidden, projector):
    tokens, width = dy.shape
    slots, features = hidden.shape
    rank = projector.shape[1]
    slab = width // GZ
    half = slab // 2
    dma = pltpu.SemaphoreType.DMA
    return pl.pallas_call(
        grad_kernel,
        out_shape=jax.ShapeDtypeStruct((half, rank), F32),
        in_specs=[
            pl.BlockSpec(memory_space=pl.ANY),
            pl.BlockSpec(memory_space=pltpu.VMEM),
            pl.BlockSpec(memory_space=pltpu.VMEM),
            pl.BlockSpec(memory_space=pl.ANY),
            pl.BlockSpec(memory_space=pl.ANY),
        ],
        out_specs=pl.BlockSpec(memory_space=pltpu.VMEM),
        scratch_shapes=[
            pltpu.VMEM((GZ, tokens, slab), BF16),
            pltpu.VMEM((slots, features), BF16),
            pltpu.VMEM((features, rank), BF16),
            pltpu.VMEM((EXPERTS * CAP, tokens), BF16),
            pltpu.VMEM((GZ, 2, GY, GX, CAP, half), BF16),
            pltpu.VMEM((GY, GX, CAP, rank), BF16),
            pltpu.VMEM((2, 2, 2, 4, CAP, rank), BF16),
            pltpu.VMEM((2, 2, rank, 8 * CAP), BF16),
            pltpu.VMEM((GZ, 2, 2, 2, 4, CAP, half), BF16),
            pltpu.VMEM((7, 2, 2, rank, half), BF16),
            pltpu.VMEM((2, 4, 2, 2, rank, half), BF16),
            pltpu.VMEM((2, 2, rank, half), BF16),
            pltpu.VMEM((4, rank, half), BF16),
            dma((2,)),
            dma((GZ,)),
            dma((2, 4)),
            dma((2, 2, 2)),
            dma((GZ, 2, 8)),
            dma((GZ, 2)),
            dma((7, 2, 2)),
            dma((2, 4, 2, 2)),
            dma((2, 2)),
            dma((4,)),
        ],
        compiler_params=pltpu.CompilerParams(
            collective_id=0, has_side_effects=True, vmem_limit_bytes=58 * 2**20
        ),
        cost_estimate=pl.CostEstimate(flops=8 * 10**9, bytes_accessed=8 * 2**20, transcendentals=0),
    )(dy, routes, gates, hidden, projector)


def update_kernel(grad, one, two, projector, weights, new_weights, new_one, new_two):
    g = grad[...]
    first = beta_one * one[:, 0, :] + (1.0 - beta_one) * g
    second = beta_two * two[:, 0, :] + (1.0 - beta_two) * g * g
    new_one[:, 0, :] = first
    new_two[:, 0, :] = second
    direction = (first / (jnp.sqrt(second) + eps)).astype(BF16)
    for at in range(0, weights.shape[0], 256):
        rows = slice(at, at + 256)
        change = dot_nt(projector[rows, :], direction)
        new_weights[rows, :] = (weights[rows, :].astype(F32) - step_size * change).astype(BF16)


def update(grad, one, two, projector, weights):
    return pl.pallas_call(
        update_kernel,
        out_shape=(
            jax.ShapeDtypeStruct(weights.shape, BF16),
            jax.ShapeDtypeStruct(one.shape, F32),
            jax.ShapeDtypeStruct(two.shape, F32),
        ),
        compiler_params=pltpu.CompilerParams(vmem_limit_bytes=32 * 2**20),
    )(grad, one, two, projector, weights)


def body(dy_tokens, gates, routes, hidden, projector, weights, moment_one, moment_two):
    projector = projector[0]
    grad = grads(dy_tokens, routes.T, gates.T, hidden[0], projector)
    new_weights, new_one, new_two = update(grad, moment_one, moment_two, projector, weights[0])
    return (new_weights[None], new_one, new_two)


def solution(mesh):
    in_specs = (
        P(("dp", "expert"), None),
        P(("dp", "expert"), None),
        P(("dp", "expert"), None),
        P("expert", "dp", None),
        P("expert", None, None),
        P("expert", None, "dp"),
        P("dp", "expert", None),
        P("dp", "expert", None),
    )
    out_specs = (P("expert", None, "dp"), P("dp", "expert", None), P("dp", "expert", None))
    return jax.shard_map(body, mesh=mesh, in_specs=in_specs, out_specs=out_specs, check_vma=False)
```

time: 300 us -> 82.2 us (0.27)
  waiting for transfers between devices: 116 us -> 0 us
  blocking collectives: 102 us -> 0 us
  Pallas kernels: 0 us -> 80.2 us
  local copies, waits for them, and re-layouts: 36.7 us -> 0.96 us
  other arithmetic: 16.5 us -> 0 us
  between operations: 14.1 us -> 0.71 us
  matrix products: 13.3 us -> 0 us
    psum x1 -> x0, waiting for transfers between devices: 116 us -> none  [body(): summed = lax.psum(grads, 'dp')]
    all_to_all x1 -> x0, blocking collectives: 102 us -> none  [body(): lax.all_to_all(outgoing, 'expert', split_axis=0, concat_axis=0, tiled=True)]
    pallas_call x0 -> x2, Pallas kernels: none -> 80.2 us  [the longest x1 78.5 us: grads(): pl.pallas_call(grad_kernel, out_shape=jax.ShapeDtypeStruct((half, rank),...]
    gather x4 -> x0, local copies, waits for them, and re-layouts: 25.3 us -> none  [the longest x1 17.8 us: pack_rows(): return (dy_tokens[taken] * factor[:, :, None]).astype(jnp.bfloat16)]
    dot_general x2 -> x0, matrix products: 13.3 us -> none  [the longest x1 10.4 us: body(): jnp.einsum('sjcd,jscr->djr', arrived, reduced, preferred_element_type=jnp...]
    convert_element_type x2 -> x0, other arithmetic: 10.7 us -> none  [the longest x1 9.97 us: pack_rows(): return (dy_tokens[taken] * factor[:, :, None]).astype(jnp.bfloat16)]
    unnamed x8 -> x10, local copies, waits for them, and re-layouts: 11 us -> 0.96 us
  transfers between devices with their start and end apart: 1 -> 0, of which waited for: 1 -> 0; matrix products, arithmetic and copies ran while one was open for 2% -> 0% of each run, Pallas kernels for 0% -> 0%
where the time goes in v1:
time: 82.2 us; the launch traced here: 81.9 us
  Pallas kernels  80.2 us (98%)
  local copies, waits for them, and re-layouts  0.96 us (1%)
    pallas_call x1, Pallas kernels, grads(): pl.pallas_call(grad_kernel, out_shape=jax.ShapeDtypeStruct((half, rank),...  78.5 us
    pallas_call x1, Pallas kernels, update(): pl.pallas_call(update_kernel, out_shape=(jax.ShapeDtypeStruct(weights.sha...  1.73 us

profile of v1, /device:TPU:1, one launch (start us, length us, event | category | flops | bytes accessed | tf_op | source)
XLA Modules:
  0.0 81.9 jit_solution(13642603464967360417)
XLA Ops:
  0.6 0.0 copy-start
  0.6 0.0 copy-start.1
  0.7 0.0 copy-start.2
  0.7 0.0 copy-start.3
  0.7 78.5 %shard_map.103.grad = f32[256,256]{1,0:T(8,128)} custom-call(bf16[512,4096]{1,0:T(8,128)(2,1)} %dy.1, s32[8,512]{1,0:T(8,128)} %bitcast.11, bf16[8,512]{1,0:T(8,128)(2,1)} %bitcast.12, bf16[1024,1536]{1,0:T(8,128)(2,1)} %bitcast.9, bf16[1536,256]{1,0:T(8,128)(2,1)} %bitcast.6), custom_call_target="tpu_custom_call" | custom-call | flops 8000000000 | bytes 8388608 | tf_op jit(solution)/shard_map/pallas_call | solution.py:245
  79.2 0.0 copy-done
  79.2 0.0 copy-done.1
  79.2 0.0 copy-done.2
  79.2 0.0 copy-done.3
  79.2 0.0 copy-start.4
  79.2 0.9 %copy-done.4 = f32[256,256]{1,0:T(8,128)S(1)} copy-done((f32[256,256]{1,0:T(8,128)S(1)}, f32[256,256]{1,0:T(8,128)}, u32[]{:S(2)}) %copy-start.4) | copy-done | bytes 262168
  80.2 1.7 %shard_map.104 = (bf16[1536,256]{1,0:T(8,128)(2,1)}, f32[256,1,256]{2,1,0:T(1,128)}, f32[256,1,256]{2,1,0:T(1,128)}) custom-call(f32[256,256]{1,0:T(8,128)S(1)} %copy-done.4, f32[256,1,256]{2,1,0:T(1,128)S(1)} %copy-done.2, f32[256,1,256]{2,1,0:T(1,128)S(1)} %copy-done.3, bf16[1536,256]{1,0:T(8,128)(2,1)S(1)} %bitcast.7, bf16[1536,256]{1,0:T(8,128)(2,1)S(1)} %bitcast.8), custom_call_target="tpu_custom_call" | custom-call | tf_op jit(solution)/shard_map/pallas_call | solution.py:302
Async XLA Ops:
  0.6 78.6 %copy-start = (bf16[1,1536,256]{2,1,0:T(8,128)(2,1)S(1)}, bf16[1,1536,256]{2,1,0:T(8,128)(2,1)}, u32[]{:S(2)}) copy-start(bf16[1,1536,256]{2,1,0:T(8,128)(2,1)} %param.12) | copy-start | bytes 2359300
  0.6 78.6 %copy-start.1 = (bf16[1,1536,256]{2,1,0:T(8,128)(2,1)S(1)}, bf16[1,1536,256]{2,1,0:T(8,128)(2,1)}, u32[]{:S(2)}) copy-start(bf16[1,1536,256]{2,1,0:T(8,128)(2,1)} %param.13) | copy-start | bytes 2359300
  0.7 78.6 %copy-start.2 = (f32[256,1,256]{2,1,0:T(1,128)S(1)}, f32[256,1,256]{2,1,0:T(1,128)}, u32[]{:S(2)}) copy-start(f32[256,1,256]{2,1,0:T(1,128)} %one.1) | copy-start | bytes 786436
  0.7 78.6 %copy-start.3 = (f32[256,1,256]{2,1,0:T(1,128)S(1)}, f32[256,1,256]{2,1,0:T(1,128)}, u32[]{:S(2)}) copy-start(f32[256,1,256]{2,1,0:T(1,128)} %two.1) | copy-start | bytes 786436
  79.2 1.0 %copy-start.4 = (f32[256,256]{1,0:T(8,128)S(1)}, f32[256,256]{1,0:T(8,128)}, u32[]{:S(2)}) copy-start(f32[256,256]{1,0:T(8,128)} %shard_map.103.grad) | copy-start | bytes 786436

commit v2 on v1

v2 whole, which is shorter than its diff:
```python
import jax
import jax.numpy as jnp
from jax import lax
from jax.experimental import pallas as pl
from jax.experimental.pallas import tpu as pltpu
from jax.sharding import PartitionSpec as P

EXPERTS = 16
CAP = 64
GX, GY, GZ = 4, 4, 8
LEAD = 3
PIECES = 2
MESH = pl.DeviceIdType.MESH

beta_one = 0.9
beta_two = 0.999
eps = 1e-06
step_size = 0.02

F32, BF16 = jnp.float32, jnp.bfloat16


def dot(a, b):
    return jnp.dot(a, b, preferred_element_type=F32)


def dot_nt(a, b):
    return lax.dot_general(a, b, (((1,), (1,)), ((), ())), preferred_element_type=F32)


def eye(n):
    same = lax.broadcasted_iota(jnp.int32, (n, n), 0) == lax.broadcasted_iota(jnp.int32, (n, n), 1)
    return jnp.where(same, 1.0, 0.0).astype(BF16)


SPOTS = ((0, 0), (1, 1), (3, 2), (2, 3))
TAKES = (
    ((0, 0), (0, 1), (0, 3), (3, 0)),
    ((1, 1), (1, 0), (1, 2), (2, 1)),
    ((3, 2), (0, 2), (2, 2), (3, 1)),
    ((2, 3), (1, 3), (2, 0), (3, 3)),
)


def grad_kernel(
    dy, routes, gates, hidden, projector, grad,
    dyb, hid, proj, pmat, pk, rl, ra, rt, rx, zs, zr, fs, fr,
    load_sem, dy_sem, r_send, r_recv, pk_send, rx_recv, z_send, z_recv, f_send, f_recv,
):
    dp, ex = lax.axis_index("dp"), lax.axis_index("expert")
    x, y, z, c = ex % GX, ex // GX, dp // 2, dp % 2

    def dev(x, y, z, c):
        return (z * 2 + c, y * GX + x)

    def near(dx, dy, c):
        return dev((x + dx) % GX, (y + dy) % GY, z, c)

    def remote(src, dst, send, recv, to):
        return pltpu.make_async_remote_copy(src, dst, send, recv, device_id=to, device_id_type=MESH)

    def landed(buf, sem):
        pltpu.make_async_copy(buf, buf, sem).wait()

    def far(s):
        return (8 - s) // 2

    def way_of(s, h):
        return (s + h) % 2

    def load_dy(s, h):
        half = dyb.shape[2] // 2
        slab = (z + jnp.where(way_of(s, h) == 0, far(s), GZ - far(s))) % GZ
        at = pl.multiple_of((slab * 2 + h) * half, half)
        return pltpu.make_async_copy(
            dy.at[:, pl.ds(at, half)], dyb.at[s, :, pl.ds(h * half, half)], dy_sem.at[s, h]
        )

    def load_hid(spot, j):
        dx, ddy = TAKES[spot][j]
        block = (y + ddy) % GY * GX + (x + dx) % GX
        return pltpu.make_async_copy(
            hidden.at[pl.ds(pl.multiple_of(block * CAP, CAP), CAP)], hid.at[spot, pl.ds(j * CAP, CAP)], load_sem.at[spot, j]
        )

    load_proj = pltpu.make_async_copy(projector, proj, load_sem.at[4, 0])
    for h in range(2):
        load_dy(0, h).start()
    load_proj.start()
    for spot in (0, 2, 1, 3):
        for j in range(4):
            load_hid(spot, j).start()

    @pl.loop(1, GZ)
    def _(s):
        for h in range(2):
            load_dy(s, h).start()

    barrier = pltpu.get_barrier_semaphore()
    steps = [(1, 0), (3, 0), (0, 1), (0, 3)]
    for dx, ddy in SPOTS[1:]:
        steps += [(dx, ddy), ((GX - dx) % GX, (GY - ddy) % GY)]
    partners = [near(dx, ddy, core) for dx, ddy in steps for core in range(2)] + [dev(x, y, z, 1 - c)]
    partners += [dev(x, y, (z + 1) % GZ, c), dev(x, y, (z + GZ - 1) % GZ, c)]
    for to in partners:
        pl.semaphore_signal(barrier, inc=1, device_id=to, device_id_type=MESH)

    zr[0, 3, 1] = jnp.zeros(zr.shape[3:], BF16)
    zr[1, 3, 0] = jnp.zeros(zr.shape[3:], BF16)

    tokens = routes.shape[1]
    ids = routes[...]
    here = ids < EXPERTS
    expert = jnp.sum(jnp.where(here, ids, 0), axis=0, keepdims=True)
    gate = jnp.sum(jnp.where(here, gates[...].astype(F32), 0.0), axis=0, keepdims=True)
    chosen = lax.broadcasted_iota(jnp.int32, (EXPERTS, tokens), 0) == expert
    earlier = lax.broadcasted_iota(jnp.int32, (tokens, tokens), 0) < lax.broadcasted_iota(
        jnp.int32, (tokens, tokens), 1
    )
    count = dot(jnp.where(chosen, 1.0, 0.0).astype(BF16), jnp.where(earlier, 1.0, 0.0).astype(BF16))
    rank = jnp.sum(jnp.where(chosen, count, 0.0), axis=0, keepdims=True).astype(jnp.int32)
    slot = expert * CAP + rank
    for e in range(0, EXPERTS, 4):
        at = lax.broadcasted_iota(jnp.int32, (4 * CAP, tokens), 0) + e * CAP
        pmat[e * CAP : (e + 4) * CAP, :] = jnp.where(at == slot, gate, 0.0).astype(BF16)

    def pack(s):
        for h in range(2):
            load_dy(s, h).wait()
        pk[s] = dot(pmat[...], dyb[s]).astype(BF16).reshape(pk.shape[1:])

    def row_copy(s, spot, j):
        (sx, sy), (bx, by) = SPOTS[spot], TAKES[spot][j]
        e = (y + GY - by) % GY * GX + (x + GX - bx) % GX
        to = near((sx - bx) % GX, (sy - by) % GY, spot // 2)
        return pk.at[s, e], rx.at[s, spot % 2, c, j], pk_send.at[s, spot, j], rx_recv.at[s, spot % 2], to

    def send(copy, stays):
        src, dst, ss, rs, to = copy
        if stays is None:
            remote(src, dst, ss, rs, to).start()
        else:
            pl.when(stays)(lambda: pltpu.make_async_copy(src, dst, rs).start())
            pl.when(jnp.logical_not(stays))(lambda: remote(src, dst, ss, rs, to).start())

    def pieces(copy):
        src, dst, ss, rs, to = copy
        step = src.shape[0] // PIECES
        for n in range(PIECES):
            part = pl.ds(n * step, step)
            yield src.at[part], dst.at[part], ss.at[n], rs, to

    def sent(copy, stays):
        src, dst, ss, rs, to = copy
        if stays is None:
            remote(src, dst, ss, rs, to).wait_send()
        else:
            pl.when(jnp.logical_not(stays))(lambda: remote(src, dst, ss, rs, to).wait_send())

    def row_stays(spot, j):
        return c == spot // 2 if j == 0 else None

    def send_rows(s, e):
        for j in (1, 2, 3, 0):
            for spot in (e, e + 2):
                send(row_copy(s, spot, j), row_stays(spot, j))

    def reduced_copy(spot):
        to = near(*SPOTS[spot], spot // 2)
        return rl.at[spot], ra.at[spot % 2, c], r_send.at[spot], r_recv.at[spot % 2, c], to

    def reduced_stays(spot):
        return c == 0 if spot == 0 else None

    load_proj.wait()
    for e in range(2):
        for spot in (e, e + 2):
            for j in range(4):
                load_hid(spot, j).wait()
            rl[spot] = dot(hid[spot], proj[...]).astype(BF16).reshape(rl.shape[1:])
        if e == 0:
            pl.semaphore_wait(barrier, len(partners))
        for spot in (e, e + 2):
            for part in pieces(reduced_copy(spot)):
                send(part, reduced_stays(spot))
        if e == 0:
            pack(0)
        send_rows(0, e)

    @pl.loop(1, LEAD)
    def _(s):
        pack(s)
        for e in range(2):
            send_rows(s, e)

    def reduced_landed(e):
        for k in range(2):
            landed(ra.at[e, k], r_recv.at[e, k])
        got = ra[e].reshape(8 * CAP, ra.shape[-1])
        rt[e] = dot_nt(eye(got.shape[1]), got).astype(BF16)

    def partial(s, e):
        landed(rx.at[s, e], rx_recv.at[s, e])
        got = rx[s, e]
        total = dot(rt[e], got.reshape(8 * CAP, got.shape[-1]))
        half = total.shape[1] // 2
        return total[:, :half], total[:, half:]

    def z_copy(s, h, e, way, k):
        to = dev(x, y, (z + jnp.where(way == 0, 1, GZ - 1)) % GZ, c)
        return remote(
            zs.at[s, h, e], zr.at[way, k - 1, h, e], z_send.at[s, h, e], z_recv.at[way, k - 1, h, e], to
        )

    for e in range(2):
        reduced_landed(e)
        halves = partial(0, e)
        for h in range(2):
            zs[0, h, e] = halves[h].astype(BF16)
            z_copy(0, h, e, h, 4).start()
    pack(LEAD)
    for e in range(2):
        send_rows(LEAD, e)

    def pass_on(s):
        k = far(s)
        for e in range(2):
            halves = partial(s, e)
            for h in range(2):
                way = way_of(s, h)

                @pl.when(s != 1)
                def _():
                    landed(zr.at[way, k, h, e], z_recv.at[way, k, h, e])

                zs[s, h, e] = (halves[h] + zr[way, k, h, e].astype(F32)).astype(BF16)
                z_copy(s, h, e, way, k).start()

    @pl.loop(1, GZ - LEAD)
    def _(s):
        pass_on(s)
        pack(s + LEAD)
        for e in range(2):
            send_rows(s + LEAD, e)

    @pl.loop(GZ - LEAD, GZ - 1)
    def _(s):
        pass_on(s)

    def owner_copy(h, e):
        sx, sy = (jnp.where(c == 0, SPOTS[e][i], SPOTS[2 + e][i]) for i in range(2))
        to = near(GX - sx, GY - sy, h)
        return fs.at[h, e], fr.at[2 * c + e], f_send.at[h, e], f_recv.at[2 * c + e], to

    def owner_stays(h, e):
        return c == 0 if h == 0 and e == 0 else None

    for e in range(2):
        halves = partial(GZ - 1, e)
        for h in range(2):
            total = halves[h]
            for way in range(2):
                landed(zr.at[way, 0, h, e], z_recv.at[way, 0, h, e])
                total = total + zr[way, 0, h, e].astype(F32)
            fs[h, e] = total.astype(BF16)
            for part in pieces(owner_copy(h, e)):
                send(part, owner_stays(h, e))

    for spot in range(4):
        for part in pieces(reduced_copy(spot)):
            sent(part, reduced_stays(spot))

    @pl.loop(0, GZ)
    def _(s):
        for spot in range(4):
            for j in range(4):
                sent(row_copy(s, spot, j), row_stays(spot, j))

    @pl.loop(0, GZ - 1)
    def _(s):
        for h in range(2):
            for e in range(2):
                z_copy(s, h, e, 0, 1).wait_send()

    for k in range(4):
        landed(fr.at[k], f_recv.at[k])
    total = fr[0].astype(F32)
    for k in range(1, 4):
        total = total + fr[k].astype(F32)
    grad[...] = total.T

    for h in range(2):
        for e in range(2):
            for part in pieces(owner_copy(h, e)):
                sent(part, owner_stays(h, e))


def grads(dy, routes, gates, hidden, projector):
    tokens, width = dy.shape
    slots, features = hidden.shape
    rank = projector.shape[1]
    slab = width // GZ
    half = slab // 2
    dma = pltpu.SemaphoreType.DMA
    return pl.pallas_call(
        grad_kernel,
        out_shape=jax.ShapeDtypeStruct((half, rank), F32),
        in_specs=[
            pl.BlockSpec(memory_space=pl.ANY),
            pl.BlockSpec(memory_space=pltpu.VMEM),
            pl.BlockSpec(memory_space=pltpu.VMEM),
            pl.BlockSpec(memory_space=pl.ANY),
            pl.BlockSpec(memory_space=pl.ANY),
        ],
        out_specs=pl.BlockSpec(memory_space=pltpu.VMEM),
        scratch_shapes=[
            pltpu.VMEM((GZ, tokens, slab), BF16),
            pltpu.VMEM((4, 4 * CAP, features), BF16),
            pltpu.VMEM((features, rank), BF16),
            pltpu.VMEM((EXPERTS * CAP, tokens), BF16),
            pltpu.VMEM((GZ, EXPERTS, CAP, slab), BF16),
            pltpu.VMEM((4, 4, CAP, rank), BF16),
            pltpu.VMEM((2, 2, 4, CAP, rank), BF16),
            pltpu.VMEM((2, rank, 8 * CAP), BF16),
            pltpu.VMEM((GZ, 2, 2, 4, CAP, slab), BF16),
            pltpu.VMEM((GZ - 1, 2, 2, rank, half), BF16),
            pltpu.VMEM((2, 4, 2, 2, rank, half), BF16),
            pltpu.VMEM((2, 2, rank, half), BF16),
            pltpu.VMEM((4, rank, half), BF16),
            dma((5, 4)),
            dma((GZ, 2)),
            dma((4, PIECES)),
            dma((2, 2)),
            dma((GZ, 4, 4)),
            dma((GZ, 2)),
            dma((GZ - 1, 2, 2)),
            dma((2, 4, 2, 2)),
            dma((2, 2, PIECES)),
            dma((4,)),
        ],
        compiler_params=pltpu.CompilerParams(
            collective_id=0, has_side_effects=True, vmem_limit_bytes=58 * 2**20
        ),
        cost_estimate=pl.CostEstimate(flops=8 * 10**9, bytes_accessed=8 * 2**20, transcendentals=0),
    )(dy, routes, gates, hidden, projector)


def update_kernel(grad, one, two, projector, weights, new_weights, new_one, new_two):
    g = grad[...]
    first = beta_one * one[:, 0, :] + (1.0 - beta_one) * g
    second = beta_two * two[:, 0, :] + (1.0 - beta_two) * g * g
    new_one[:, 0, :] = first
    new_two[:, 0, :] = second
    direction = (first / (jnp.sqrt(second) + eps)).astype(BF16)
    for at in range(0, weights.shape[0], 256):
        rows = slice(at, at + 256)
        change = dot_nt(projector[rows, :], direction)
        new_weights[rows, :] = (weights[rows, :].astype(F32) - step_size * change).astype(BF16)


def update(grad, one, two, projector, weights):
    return pl.pallas_call(
        update_kernel,
        out_shape=(
            jax.ShapeDtypeStruct(weights.shape, BF16),
            jax.ShapeDtypeStruct(one.shape, F32),
            jax.ShapeDtypeStruct(two.shape, F32),
        ),
        compiler_params=pltpu.CompilerParams(vmem_limit_bytes=32 * 2**20),
    )(grad, one, two, projector, weights)


def body(dy_tokens, gates, routes, hidden, projector, weights, moment_one, moment_two):
    projector = projector[0]
    grad = grads(dy_tokens, routes.T, gates.T, hidden[0], projector)
    new_weights, new_one, new_two = update(grad, moment_one, moment_two, projector, weights[0])
    return (new_weights[None], new_one, new_two)


def solution(mesh):
    in_specs = (
        P(("dp", "expert"), None),
        P(("dp", "expert"), None),
        P(("dp", "expert"), None),
        P("expert", "dp", None),
        P("expert", None, None),
        P("expert", None, "dp"),
        P("dp", "expert", None),
        P("dp", "expert", None),
    )
    out_specs = (P("expert", None, "dp"), P("dp", "expert", None), P("dp", "expert", None))
    return jax.shard_map(body, mesh=mesh, in_specs=in_specs, out_specs=out_specs, check_vma=False)
```

time: 82.2 us -> 77.8 us (0.946)
  Pallas kernels: 80.2 us -> 76 us
    pallas_call x1, Pallas kernels: 78.5 us -> 74.2 us  [grads(): pl.pallas_call(grad_kernel, out_shape=jax.ShapeDtypeStruct((half, rank),...]
where the time goes in v2:
time: 77.8 us; the launch traced here: 77.6 us
  Pallas kernels  76 us (98%)
  local copies, waits for them, and re-layouts  0.96 us (1%)
    pallas_call x1, Pallas kernels, grads(): pl.pallas_call(grad_kernel, out_shape=jax.ShapeDtypeStruct((half, rank),...  74.2 us
    pallas_call x1, Pallas kernels, update(): pl.pallas_call(update_kernel, out_shape=(jax.ShapeDtypeStruct(weights.sha...  1.74 us

profile of v2, /device:TPU:1, one launch (start us, length us, event | category | flops | bytes accessed | tf_op | source)
XLA Modules:
  0.0 77.6 jit_solution(8136452062084923843)
XLA Ops:
  0.6 0.0 copy-start
  0.6 0.0 copy-start.1
  0.7 0.0 copy-start.2
  0.7 0.0 copy-start.3
  0.7 74.2 %shard_map.103.grad = f32[256,256]{1,0:T(8,128)} custom-call(bf16[512,4096]{1,0:T(8,128)(2,1)} %dy.1, s32[8,512]{1,0:T(8,128)} %bitcast.11, bf16[8,512]{1,0:T(8,128)(2,1)} %bitcast.12, bf16[1024,1536]{1,0:T(8,128)(2,1)} %bitcast.9, bf16[1536,256]{1,0:T(8,128)(2,1)} %bitcast.6), custom_call_target="tpu_custom_call" | custom-call | flops 8000000000 | bytes 8388608 | tf_op jit(solution)/shard_map/pallas_call | solution.py:305
  74.9 0.0 copy-done
  74.9 0.0 copy-done.1
  74.9 0.0 copy-done.2
  74.9 0.0 copy-done.3
  74.9 0.0 copy-start.4
  75.0 0.9 %copy-done.4 = f32[256,256]{1,0:T(8,128)S(1)} copy-done((f32[256,256]{1,0:T(8,128)S(1)}, f32[256,256]{1,0:T(8,128)}, u32[]{:S(2)}) %copy-start.4) | copy-done | bytes 262168
  75.9 1.7 %shard_map.104 = (bf16[1536,256]{1,0:T(8,128)(2,1)}, f32[256,1,256]{2,1,0:T(1,128)}, f32[256,1,256]{2,1,0:T(1,128)}) custom-call(f32[256,256]{1,0:T(8,128)S(1)} %copy-done.4, f32[256,1,256]{2,1,0:T(1,128)S(1)} %copy-done.2, f32[256,1,256]{2,1,0:T(1,128)S(1)} %copy-done.3, bf16[1536,256]{1,0:T(8,128)(2,1)S(1)} %bitcast.7, bf16[1536,256]{1,0:T(8,128)(2,1)S(1)} %bitcast.8), custom_call_target="tpu_custom_call" | custom-call | tf_op jit(solution)/shard_map/pallas_call | solution.py:362
Async XLA Ops:
  0.6 74.3 %copy-start = (bf16[1,1536,256]{2,1,0:T(8,128)(2,1)S(1)}, bf16[1,1536,256]{2,1,0:T(8,128)(2,1)}, u32[]{:S(2)}) copy-start(bf16[1,1536,256]{2,1,0:T(8,128)(2,1)} %param.12) | copy-start | bytes 2359300
  0.6 74.3 %copy-start.1 = (bf16[1,1536,256]{2,1,0:T(8,128)(2,1)S(1)}, bf16[1,1536,256]{2,1,0:T(8,128)(2,1)}, u32[]{:S(2)}) copy-start(bf16[1,1536,256]{2,1,0:T(8,128)(2,1)} %param.13) | copy-start | bytes 2359300
  0.7 74.3 %copy-start.2 = (f32[256,1,256]{2,1,0:T(1,128)S(1)}, f32[256,1,256]{2,1,0:T(1,128)}, u32[]{:S(2)}) copy-start(f32[256,1,256]{2,1,0:T(1,128)} %one.1) | copy-start | bytes 786436
  0.7 74.3 %copy-start.3 = (f32[256,1,256]{2,1,0:T(1,128)S(1)}, f32[256,1,256]{2,1,0:T(1,128)}, u32[]{:S(2)}) copy-start(f32[256,1,256]{2,1,0:T(1,128)} %two.1) | copy-start | bytes 786436
  74.9 1.0 %copy-start.4 = (f32[256,256]{1,0:T(8,128)S(1)}, f32[256,256]{1,0:T(8,128)}, u32[]{:S(2)}) copy-start(f32[256,256]{1,0:T(8,128)} %shard_map.103.grad) | copy-start | bytes 786436

commit v3 on v2

--- a/solution.py
+++ b/solution.py
@@ -8,7 +8,7 @@
 EXPERTS = 16
 CAP = 64
 GX, GY, GZ = 4, 4, 8
-LEAD = 3
+LEAD = 2
 PIECES = 2
 MESH = pl.DeviceIdType.MESH
 
@@ -190,7 +190,7 @@
     @pl.loop(1, LEAD)
     def _(s):
         pack(s)
-        for e in range(2):
+        for e in (1, 0):
             send_rows(s, e)
 
     def reduced_landed(e):
@@ -219,12 +219,12 @@
             zs[0, h, e] = halves[h].astype(BF16)
             z_copy(0, h, e, h, 4).start()
     pack(LEAD)
-    for e in range(2):
+    for e in (1, 0):
         send_rows(LEAD, e)
 
     def pass_on(s):
         k = far(s)
-        for e in range(2):
+        for e in (1, 0):
             halves = partial(s, e)
             for h in range(2):
                 way = way_of(s, h)
@@ -240,7 +240,7 @@
     def _(s):
         pass_on(s)
         pack(s + LEAD)
-        for e in range(2):
+        for e in (1, 0):
             send_rows(s + LEAD, e)
 
     @pl.loop(GZ - LEAD, GZ - 1)
@@ -255,7 +255,7 @@
     def owner_stays(h, e):
         return c == 0 if h == 0 and e == 0 else None
 
-    for e in range(2):
+    for e in (1, 0):
         halves = partial(GZ - 1, e)
         for h in range(2):
             total = halves[h]

time: 77.8 us -> 78 us (level)
  no operation moved by 1% of the time
where the time goes in v3:
time: 78 us; the launch traced here: 77.8 us
  Pallas kernels  76.2 us (98%)
  local copies, waits for them, and re-layouts  0.96 us (1%)
    pallas_call x1, Pallas kernels, grads(): pl.pallas_call(grad_kernel, out_shape=jax.ShapeDtypeStruct((half, rank),...  74.4 us
    pallas_call x1, Pallas kernels, update(): pl.pallas_call(update_kernel, out_shape=(jax.ShapeDtypeStruct(weights.sha...  1.73 us

profile of v3, /device:TPU:1, one launch (start us, length us, event | category | flops | bytes accessed | tf_op | source)
XLA Modules:
  0.0 77.8 jit_solution(6753742254741700160)
XLA Ops:
  0.6 0.0 copy-start
  0.6 0.0 copy-start.1
  0.7 0.0 copy-start.2
  0.7 0.0 copy-start.3
  0.7 74.4 %shard_map.103.grad = f32[256,256]{1,0:T(8,128)} custom-call(bf16[512,4096]{1,0:T(8,128)(2,1)} %dy.1, s32[8,512]{1,0:T(8,128)} %bitcast.11, bf16[8,512]{1,0:T(8,128)(2,1)} %bitcast.12, bf16[1024,1536]{1,0:T(8,128)(2,1)} %bitcast.9, bf16[1536,256]{1,0:T(8,128)(2,1)} %bitcast.6), custom_call_target="tpu_custom_call" | custom-call | flops 8000000000 | bytes 8388608 | tf_op jit(solution)/shard_map/pallas_call | solution.py:305
  75.1 0.0 copy-done
  75.1 0.0 copy-done.1
  75.1 0.0 copy-done.2
  75.1 0.0 copy-done.3
  75.1 0.0 copy-start.4
  75.2 0.9 %copy-done.4 = f32[256,256]{1,0:T(8,128)S(1)} copy-done((f32[256,256]{1,0:T(8,128)S(1)}, f32[256,256]{1,0:T(8,128)}, u32[]{:S(2)}) %copy-start.4) | copy-done | bytes 262168
  76.1 1.7 %shard_map.104 = (bf16[1536,256]{1,0:T(8,128)(2,1)}, f32[256,1,256]{2,1,0:T(1,128)}, f32[256,1,256]{2,1,0:T(1,128)}) custom-call(f32[256,256]{1,0:T(8,128)S(1)} %copy-done.4, f32[256,1,256]{2,1,0:T(1,128)S(1)} %copy-done.2, f32[256,1,256]{2,1,0:T(1,128)S(1)} %copy-done.3, bf16[1536,256]{1,0:T(8,128)(2,1)S(1)} %bitcast.7, bf16[1536,256]{1,0:T(8,128)(2,1)S(1)} %bitcast.8), custom_call_target="tpu_custom_call" | custom-call | tf_op jit(solution)/shard_map/pallas_call | solution.py:362
Async XLA Ops:
  0.6 74.5 %copy-start = (bf16[1,1536,256]{2,1,0:T(8,128)(2,1)S(1)}, bf16[1,1536,256]{2,1,0:T(8,128)(2,1)}, u32[]{:S(2)}) copy-start(bf16[1,1536,256]{2,1,0:T(8,128)(2,1)} %param.12) | copy-start | bytes 2359300
  0.6 74.5 %copy-start.1 = (bf16[1,1536,256]{2,1,0:T(8,128)(2,1)S(1)}, bf16[1,1536,256]{2,1,0:T(8,128)(2,1)}, u32[]{:S(2)}) copy-start(bf16[1,1536,256]{2,1,0:T(8,128)(2,1)} %param.13) | copy-start | bytes 2359300
  0.7 74.5 %copy-start.2 = (f32[256,1,256]{2,1,0:T(1,128)S(1)}, f32[256,1,256]{2,1,0:T(1,128)}, u32[]{:S(2)}) copy-start(f32[256,1,256]{2,1,0:T(1,128)} %one.1) | copy-start | bytes 786436
  0.7 74.5 %copy-start.3 = (f32[256,1,256]{2,1,0:T(1,128)S(1)}, f32[256,1,256]{2,1,0:T(1,128)}, u32[]{:S(2)}) copy-start(f32[256,1,256]{2,1,0:T(1,128)} %two.1) | copy-start | bytes 786436
  75.1 1.0 %copy-start.4 = (f32[256,256]{1,0:T(8,128)S(1)}, f32[256,256]{1,0:T(8,128)}, u32[]{:S(2)}) copy-start(f32[256,256]{1,0:T(8,128)} %shard_map.103.grad) | copy-start | bytes 786436
